TPU v7x, 768 devices: a whole 4x8x12 slice. The times are simulated.
768 devices in a mesh: dp: 64 (over x, y, core), seq: 12 (over z).
Axes of the slice: x: 4, y: 8, z: 12, core: 2. Of those that a mesh axis runs over, the one named last changes fastest.
Arguments:
- token_ids: int32 [98304], P('dp'), may hold values from 0 to 127999, as said below
- embed_table: bfloat16 [128000, 2304], P('dp', 'seq'), may hold values from -0.125 to 0.125
- second_moment: bfloat16 [128000, 2304], P('dp', 'seq'), may hold values from 0.099609375 to 4
- cotangent: bfloat16 [98304, 2304], P(('dp', 'seq')), may hold values from -0.125 to 0.125
Outputs:
- embedded: bfloat16 [98304, 2304], P(('dp', 'seq'))
- new_table: bfloat16 [128000, 2304], P('dp', 'seq')
- new_moment: bfloat16 [128000, 2304], P('dp', 'seq')
Inputs may be any that keep to these rules, and one draw needn't show every extreme that they name: `token_ids`: among the tokens of one index of dp at most 16 distinct ids lie in one block of 2000 consecutive ids; in every draw some block holds exactly 16 distinct ids of every index's tokens.
All inputs are finite; a program needn't handle non-finite values.
Results may differ from a plain program's by a relative error of at most 0.008.
Values may be sent and summed in bfloat16 or wider, within the bound.
No kernel may reach another device: no remote copies, remote signals or barrier semaphores. Data moves between devices by JAX's collectives and lax.ppermute only.
A program may use at most 64 MiB of HBM per device.

v0:
```python
import math

import jax
import jax.numpy as jnp
from jax import lax
from jax.sharding import PartitionSpec as P

D = 2304
CAP = 16
STEP = 1000


beta_two = 0.95
epsilon = 1e-08
learn_rate = 0.01
weight_decay = 0.1


def local(token_ids, embed_table, second_moment, cotangent):
    dp_count = lax.axis_size("dp")
    group_size = token_ids.shape[0]
    tok_rows = cotangent.shape[0]
    owner_rows = embed_table.shape[0]
    slot_count = dp_count * CAP
    normalizer = math.sqrt(D)
    sort_order = jnp.argsort(token_ids, stable=True)
    sorted_ids = token_ids[sort_order]
    is_first = jnp.concatenate(
        [jnp.ones((1,), jnp.int32), (sorted_ids[1:] != sorted_ids[:-1]).astype(jnp.int32)]
    )
    distinct_rank = jnp.cumsum(is_first) - 1
    owner_sorted = sorted_ids // owner_rows
    owner_match = owner_sorted[:, None] == jnp.arange(dp_count, dtype=jnp.int32)[None, :]
    per_owner = jnp.sum(jnp.where(owner_match, is_first[:, None], 0), axis=0)
    owner_base = jnp.cumsum(per_owner) - per_owner
    token_base = jnp.sum(jnp.where(owner_match, owner_base[None, :], 0), axis=1)
    slot_sorted = owner_sorted * CAP + distinct_rank - token_base
    slot_token = jnp.zeros((group_size,), jnp.int32).at[sort_order].set(slot_sorted)
    requests = (
        jnp.full((slot_count,), -1, jnp.int32)
        .at[slot_sorted]
        .set(sorted_ids - owner_sorted * owner_rows)
    )
    requests = requests.reshape(dp_count, CAP)
    columns = lax.all_to_all(cotangent, "seq", split_axis=1, concat_axis=0, tiled=True)
    incidence = (jnp.arange(slot_count, dtype=jnp.int32)[:, None] == slot_token[None, :]).astype(
        jnp.bfloat16
    )
    slot_grads = jnp.dot(incidence, columns, preferred_element_type=jnp.float32).reshape(
        dp_count, CAP, -1
    )
    received = lax.all_to_all(requests, "dp", split_axis=0, concat_axis=0, tiled=True)
    live_slot = (received >= 0).reshape(-1)
    local_rows = jnp.where(live_slot, received.reshape(-1), 0)
    picked_rows = embed_table[local_rows].reshape(dp_count, CAP, -1)
    returned_rows = lax.all_to_all(
        picked_rows, "dp", split_axis=0, concat_axis=0, tiled=True
    ).reshape(slot_count, -1)
    whole_rows = lax.all_gather(returned_rows, "seq", axis=1, tiled=True)
    own_slots = lax.dynamic_slice_in_dim(slot_token, lax.axis_index("seq") * tok_rows, tok_rows)
    embedded = (whole_rows[own_slots].astype(jnp.float32) * normalizer).astype(jnp.bfloat16)
    arrived = lax.all_to_all(
        slot_grads.astype(jnp.bfloat16), "dp", split_axis=0, concat_axis=0, tiled=True
    ).astype(slot_grads.dtype)
    flat_grads = arrived.reshape(slot_count, -1)
    target_rows = jnp.where(live_slot, local_rows, owner_rows)
    summed = jax.ops.segment_sum(flat_grads, target_rows, num_segments=owner_rows + 1)[:owner_rows]
    hit_count = jax.ops.segment_sum(
        live_slot.astype(jnp.int32), target_rows, num_segments=owner_rows + 1
    )[:owner_rows]
    touched = (hit_count > 0)[:, None]
    gradient = summed * normalizer
    weights = embed_table.astype(jnp.float32)
    moment_new = (
        beta_two * second_moment.astype(jnp.float32) + (1.0 - beta_two) * gradient * gradient
    )
    denominator = jnp.sqrt(moment_new / (1.0 - beta_two**STEP)) + epsilon
    updated = weights - learn_rate * (gradient / denominator + weight_decay * weights)
    new_table = jnp.where(touched, updated.astype(jnp.bfloat16), embed_table)
    new_moment = jnp.where(touched, moment_new.astype(jnp.bfloat16), second_moment)
    return (embedded, new_table, new_moment)


def solution(mesh):
    in_specs = (P("dp"), P("dp", "seq"), P("dp", "seq"), P(("dp", "seq"), None))
    out_specs = (P(("dp", "seq"), None), P("dp", "seq"), P("dp", "seq"))
    return jax.shard_map(local, mesh=mesh, in_specs=in_specs, out_specs=out_specs, check_vma=False)
```

profile of v0, /device:TPU:1, one launch (start us, length us, event | category | flops | bytes accessed | tf_op | source)
XLA Modules:
  0.0 187.8 jit_solution(7102439060627311711)
XLA Ops:
  7.2 5.8 %sort.17 = (s32[1536]{0:T(1024)}, s32[1536]{0:T(1024)S(1)}) sort(s32[1536]{0:T(1024)} %param.4, s32[1536]{0:T(1024)S(1)} %iota.19), dimensions={0}, to_apply=%region_0.0 | sort | flops 16896 | bytes 24576 | tf_op jit(solution)/shard_map/jit(argsort)/sort | solution.py:26
  13.0 8.4 %gather_fusion = s32[1536]{0:T(1024)S(1)} fusion(s32[1536]{0:T(1024)S(1)} %copy-done, s32[2048]{0:T(1024)S(1)} %pad_clamp_fusion), kind=kCustom, calls=%fused_computation | custom fusion | bytes 18432 | tf_op jit(solution)/shard_map/gather | solution.py:27
  21.4 0.1 slice_compare_fusion.1
  21.5 0.1 fusion.27
  21.6 0.1 select_reduce_fusion.1
  21.7 0.1 copy.47
  21.8 0.1 reduce-window.21
  21.9 0.1 reduce.1
  22.1 0.1 select_reduce_fusion
  22.2 0.3 reduce-window.19
  22.5 0.1 slice.33
  22.6 0.1 slice_reduce_fusion
  22.7 0.1 fusion.17
  22.8 0.1 fusion.15
  22.9 6.2 %scatter_custom_fusion = s32[1024]{0:T(1024)S(1)} fusion(s32[1536]{0:T(1024)S(1)} %fusion.18, s32[1536]{0:T(1024)S(1)} %get-tuple-element.23, s32[]{:T(128)} %constant.17.clone.1), kind=kCustom, calls=%fused_computation.62 | custom fusion | bytes 4100 | tf_op jit(solution)/shard_map/scatter | solution.py:42
  29.1 0.7 all_to_all.28
  29.8 14.5 %all-to-all-start = ((s32[64,1,16]{2,1,0:T(1,128)}), s32[64,1,16]{2,1,0:T(1,128)S(1)}, u32[]{:S(2)}, u32[]{:S(2)}) async-start(s32[64,1,16]{2,1,0:T(1,128)} %bitcast.2), calls=%async_computation | async-start | bytes 65536 | tf_op jit(solution)/shard_map/all_to_all | solution.py:52
  44.3 0.0 all-gather.2.cloned.1.call-start
  44.4 0.9 copy.49
  45.3 8.4 %all-to-all-done = s32[64,1,16]{2,1,0:T(1,128)S(1)} async-done(((s32[64,1,16]{2,1,0:T(1,128)}), s32[64,1,16]{2,1,0:T(1,128)S(1)}, u32[]{:S(2)}, u32[]{:S(2)}) %all-to-all-start) | async-done | bytes 4128 | tf_op jit(solution)/shard_map/all_to_all | solution.py:52
  53.7 0.5 broadcast.227
  54.2 0.8 fusion.14
  55.0 0.1 all_to_all.30
  55.1 3.9 %gather_fusion.1 = bf16[1024,192]{1,0:T(8,128)(2,1)S(1)} fusion(bf16[2000,192]{1,0:T(8,128)(2,1)S(1)} %copy.49, s32[1024]{0:T(1024)S(1)} %broadcast_clamp_fusion), kind=kCustom, calls=%fused_computation.1 | custom fusion | bytes 790528 | tf_op jit(solution)/shard_map/gather | solution.py:55
  59.1 21.4 %all_to_all.41 = bf16[64,16,192]{2,1,0:T(8,128)(2,1)S(1)} all-to-all(bf16[64,16,192]{2,1,0:T(8,128)(2,1)S(1)} %bitcast.30), channel_id=1, replica_groups=mesh['dp'=64,'seq'=12] {'dp'}, dimensions={0} | all-to-all | bytes 786432 | tf_op jit(solution)/shard_map/all_to_all | solution.py:56
  80.5 0.9 copy.50
  81.4 0.0 all-gather.2.cloned.1.call-update
  81.4 1.1 copy.53
  82.5 11.8 %all-to-all-start.2 = ((bf16[128,12,192]{0,2,1:T(8,128)(2,1)}), bf16[128,12,192]{0,2,1:T(8,128)(2,1)S(1)}, u32[]{:S(2)}, u32[]{:S(2)}) async-start(bf16[128,12,192]{0,2,1:T(8,128)(2,1)} %bitcast.8), calls=%async_computation.2 | async-start | bytes 1179648 | tf_op jit(solution)/shard_map/all_to_all | solution.py:45
  94.3 6.2 %scatter_custom_fusion.1 = s32[1536]{0:T(1024)S(1)} fusion(s32[1536]{0:T(1024)S(1)} %compare_select_fusion.2, s32[1536]{0:T(1024)S(1)} %get-tuple-element.21, s32[]{:T(128)} %constant.18.clone.1), kind=kCustom, calls=%fused_computation.58 | custom fusion | bytes 6148 | tf_op jit(solution)/shard_map/scatter | solution.py:38
  100.6 21.1 %all-to-all-done.2 = bf16[128,12,192]{0,2,1:T(8,128)(2,1)S(1)} async-done(((bf16[128,12,192]{0,2,1:T(8,128)(2,1)}), bf16[128,12,192]{0,2,1:T(8,128)(2,1)S(1)}, u32[]{:S(2)}, u32[]{:S(2)}) %all-to-all-start.2) | async-done | bytes 589856 | tf_op jit(solution)/shard_map/all_to_all | solution.py:45
  121.6 0.4 copy.54
  122.1 0.4 reshape.296
  122.5 1.9 fusion.8
  124.3 11.2 %all-to-all-start.3 = ((bf16[64,16,192]{2,1,0:T(8,128)(2,1)}), bf16[64,16,192]{2,1,0:T(8,128)(2,1)S(1)}, u32[]{:S(2)}, u32[]{:S(2)}) async-start(bf16[64,16,192]{2,1,0:T(8,128)(2,1)} %fusion.8), calls=%async_computation.3 | async-start | bytes 1048576 | tf_op jit(solution)/shard_map/all_to_all | solution.py:62
  135.6 1.4 copy.55
  137.0 0.1 compare_select_fusion.5
  137.1 0.1 reshape.281
  137.1 7.3 %scatter_custom_fusion.2 = s32[2001]{0:T(1024)S(1)} fusion(s32[1024]{0:T(1024)S(1)} %bitcast.32, s32[1024]{0:T(1024)S(1)} %reshape.281, s32[]{:T(128)} %constant.18.clone.1), kind=kCustom, calls=%fused_computation.55 | custom fusion | flops 1024 | bytes 8008 | tf_op jit(solution)/shard_map/scatter-add | solution.py:68
  144.4 8.5 %all-to-all-done.3 = bf16[64,16,192]{2,1,0:T(8,128)(2,1)S(1)} async-done(((bf16[64,16,192]{2,1,0:T(8,128)(2,1)}), bf16[64,16,192]{2,1,0:T(8,128)(2,1)S(1)}, u32[]{:S(2)}, u32[]{:S(2)}) %all-to-all-start.3) | async-done | bytes 393248 | tf_op jit(solution)/shard_map/all_to_all | solution.py:62
  152.9 0.8 copy-done.2
  153.7 6.6 %scatter_custom_fusion.3 = f32[2001,192]{1,0:T(8,128)S(1)} fusion(s32[1024]{0:T(1024)S(1)} %bitcast.33, bf16[1024,192]{1,0:T(8,128)(2,1)} %bitcast.29, f32[]{:T(128)} %constant.28.clone.1), kind=kCustom, calls=%fused_computation.21 | custom fusion | flops 393216 | bytes 1929988 | tf_op jit(solution)/shard_map/scatter-add | solution.py:67
  160.3 4.7 %convert_select_fusion = (bf16[2000,192]{1,0:T(8,128)(2,1)}, bf16[2000,192]{1,0:T(8,128)(2,1)}) fusion(bf16[2000,192]{1,0:T(8,128)(2,1)} %copy.55, f32[2001,192]{1,0:T(8,128)S(1)} %scatter_custom_fusion.3, pred[2000]{0:T(1024)(128)(4,1)S(1)} %slice_compare_fusion, bf16[2000,192]{1,0:T(8,128)(2,1)S(1)} %copy.49), kind=kLoop, calls=%fused_computation.24 | loop fusion | flops 6528000 | bytes 4610000 | tf_op jit(solution)/shard_map/jit(_where)/select_n | solution.py:80
  164.9 2.3 %copy.58 = bf16[2000,192]{0,1:T(8,128)(2,1)} copy(bf16[2000,192]{1,0:T(8,128)(2,1)} %get-tuple-element.20) | data formatting | bytes 1536000
  167.2 1.5 copy.59
  168.8 6.8 %copy.51 = bf16[1024,2304]{1,0:T(8,128)(2,1)} copy(bf16[1024,2304]{0,1:T(8,128)(2,1)} %all-gather.2.cloned.1.call-done) | data formatting | bytes 9437184 | tf_op jit(solution)/shard_map/all_gather | solution.py:59
  175.5 4.5 %gather_fusion.2 = bf16[128,2304]{1,0:T(8,128)(2,1)S(1)} fusion(bf16[1024,2304]{1,0:T(8,128)(2,1)} %copy.51, s32[1024]{0:T(1024)S(1)} %pad_clamp_fusion.1), kind=kCustom, calls=%fused_computation.2 | custom fusion | bytes 1180160 | tf_op jit(solution)/shard_map/gather | solution.py:61
  180.0 0.9 multiply_convert_fusion
  (25 shorter events, 0.2 us)
Async XLA Ops:
  7.2 5.8 %copy-start = (s32[1536]{0:T(1024)S(1)}, s32[1536]{0:T(1024)}, u32[]{:S(2)}) copy-start(s32[1536]{0:T(1024)} %param.4) | copy-start | bytes 18436
  13.0 31.4 %copy-start.3 = (bf16[2000,192]{0,1:T(8,128)(2,1)S(1)}, bf16[2000,192]{0,1:T(8,128)(2,1)}, u32[]{:S(2)}) copy-start(bf16[2000,192]{0,1:T(8,128)(2,1)} %param.5) | copy-start | bytes 2304004
  29.8 23.9 %all-to-all-start = ((s32[64,1,16]{2,1,0:T(1,128)}), s32[64,1,16]{2,1,0:T(1,128)S(1)}, u32[]{:S(2)}, u32[]{:S(2)}) async-start(s32[64,1,16]{2,1,0:T(1,128)} %bitcast.2), calls=%async_computation | async-start | bytes 65536 | tf_op jit(solution)/shard_map/all_to_all | solution.py:52
  44.3 124.4 %all-gather.2.cloned.1.call-start = ((), (), s32[]{:S(2)}) async-start(), calls=%async_computation.4 | async-start | bytes 5111808 | tf_op jit(solution)/shard_map/all_gather | solution.py:59
  59.1 22.4 %copy-start.5 = (bf16[128,2304]{1,0:T(8,128)(2,1)S(1)}, bf16[128,2304]{1,0:T(8,128)(2,1)}, u32[]{:S(2)}) copy-start(bf16[128,2304]{1,0:T(8,128)(2,1)} %param.7) | copy-start | bytes 1769476
  82.5 39.1 %all-to-all-start.2 = ((bf16[128,12,192]{0,2,1:T(8,128)(2,1)}), bf16[128,12,192]{0,2,1:T(8,128)(2,1)S(1)}, u32[]{:S(2)}, u32[]{:S(2)}) async-start(bf16[128,12,192]{0,2,1:T(8,128)(2,1)} %bitcast.8), calls=%async_computation.2 | async-start | bytes 1179648 | tf_op jit(solution)/shard_map/all_to_all | solution.py:45
  122.5 13.1 %copy-start.4 = (bf16[2000,192]{0,1:T(8,128)(2,1)S(1)}, bf16[2000,192]{0,1:T(8,128)(2,1)}, u32[]{:S(2)}) copy-start(bf16[2000,192]{0,1:T(8,128)(2,1)} %param.6) | copy-start | bytes 2304004
  124.3 28.6 %all-to-all-start.3 = ((bf16[64,16,192]{2,1,0:T(8,128)(2,1)}), bf16[64,16,192]{2,1,0:T(8,128)(2,1)S(1)}, u32[]{:S(2)}, u32[]{:S(2)}) async-start(bf16[64,16,192]{2,1,0:T(8,128)(2,1)} %fusion.8), calls=%async_computation.3 | async-start | bytes 1048576 | tf_op jit(solution)/shard_map/all_to_all | solution.py:62
  152.9 0.8 copy-start.2
  164.9 2.3 %copy-start.1 = (bf16[2000,192]{1,0:T(8,128)(2,1)S(1)}, bf16[2000,192]{1,0:T(8,128)(2,1)}, u32[]{:S(2)}) copy-start(bf16[2000,192]{1,0:T(8,128)(2,1)} %get-tuple-element.19) | copy-start | bytes 2304004
Sparse Core Ops, SparseCore 0:
  81.6 82.2 all-gather.1
where the time goes:
time: 189 us; the launch traced here: 188 us
  local copies, waits for them, and re-layouts  47.3 us (25%)
  waiting for transfers between devices  37.9 us (20%)
  starting transfers between devices  37.7 us (20%)
  other arithmetic  27.3 us (14%)
  blocking collectives  21.4 us (11%)
  between operations  14.3 us (8%)
    all_to_all x1, blocking collectives, local(): lax.all_to_all(picked_rows, 'dp', split_axis=0, concat_axis=0, tiled=True)  21.4 us
    all_to_all x1, waiting for transfers between devices, local(): lax.all_to_all(cotangent, 'seq', split_axis=1, concat_axis=0, tiled=True)  21.1 us
    all_to_all x1, starting transfers between devices, local(): lax.all_to_all(requests, 'dp', split_axis=0, concat_axis=0, tiled=True)  14.5 us
    all_to_all x1, starting transfers between devices, local(): lax.all_to_all(cotangent, 'seq', split_axis=1, concat_axis=0, tiled=True)  11.8 us
    all_to_all x1, starting transfers between devices, local(): lax.all_to_all(slot_grads.astype(jnp.bfloat16), 'dp', split_axis=0, conca...  11.2 us
    all_to_all x1, waiting for transfers between devices, local(): lax.all_to_all(slot_grads.astype(jnp.bfloat16), 'dp', split_axis=0, conca...  8.47 us
    gather x1, local copies, waits for them, and re-layouts, local(): sorted_ids = token_ids[sort_order]  8.39 us
    all_to_all x1, waiting for transfers between devices, local(): lax.all_to_all(requests, 'dp', split_axis=0, concat_axis=0, tiled=True)  8.37 us
  transfers between devices with their start and end apart: 4, of which 3 were waited for; matrix products, arithmetic and copies ran while one was open for 18% of the time, Pallas kernels for 0%

commit v1 on v0

v1 whole, which is shorter than its diff:
```python
import functools
import math

import jax
import jax.numpy as jnp
from jax import lax
from jax.experimental import pallas as pl
from jax.experimental.pallas import tpu as pltpu
from jax.sharding import PartitionSpec as P

D = 2304
CAP = 16
STEP = 1000
VOCAB_ROWS = 2000

beta_two = 0.95
epsilon = 1e-08
learn_rate = 0.01
weight_decay = 0.1

BF16 = jnp.bfloat16
F32 = jnp.float32
I32 = jnp.int32
VMEM_LIMIT = 48 * 1024 * 1024


def call(kernel, out_shape, n_in, scratch=(), smem_in=(), flops=0, nbytes=0):
    def spec(i):
        return pl.BlockSpec(memory_space=pltpu.SMEM if i in smem_in else pltpu.VMEM)

    many = isinstance(out_shape, (list, tuple))
    return pl.pallas_call(
        kernel,
        out_shape=out_shape,
        in_specs=[spec(i) for i in range(n_in)],
        out_specs=[pl.BlockSpec(memory_space=pltpu.VMEM) for _ in out_shape]
        if many
        else pl.BlockSpec(memory_space=pltpu.VMEM),
        scratch_shapes=list(scratch),
        compiler_params=pltpu.CompilerParams(vmem_limit_bytes=VMEM_LIMIT),
        cost_estimate=pl.CostEstimate(flops=flops, bytes_accessed=nbytes, transcendentals=0),
    )


def iota(shape, dim):
    return lax.broadcasted_iota(I32, shape, dim)


def pack_cotangent(cot_ref, out_ref):
    for peer in range(out_ref.shape[0]):
        block = cot_ref[:, 192 * peer : 192 * peer + 192]
        out_ref[peer, 0:128, :] = block[:, 0:128]
        out_ref[peer, 128:192, :] = jnp.concatenate(
            [block[0:64, 128:192], block[64:128, 128:192]], axis=1
        )


def unpack_tokens(in_ref, out_ref):
    for peer in range(in_ref.shape[0]):
        tail = in_ref[peer, 128:192, :]
        out_ref[:, 192 * peer : 192 * peer + 128] = in_ref[peer, 0:128, :]
        out_ref[:, 192 * peer + 128 : 192 * peer + 192] = jnp.concatenate(
            [tail[:, 0:64], tail[:, 64:128]], axis=0
        )


def columns_of(row):
    return jnp.transpose(jnp.broadcast_to(row, (128, 128)))


def number_slots(me_ref, ids_ref, slot_ref, want_ref, id_cols, first_cols, first_rows):
    blocks = ids_ref.shape[0]
    me = me_ref[0]
    ids = ids_ref[...].astype(F32)
    for i in range(blocks):
        id_cols[i] = columns_of(ids[i : i + 1, :])
    earlier = iota((128, 128), 0) < iota((128, 128), 1)
    for j in range(blocks):
        row = ids[j : j + 1, :]
        seen = jnp.where((id_cols[j] == row) & earlier, 1.0, 0.0)
        for i in range(j):
            seen = jnp.where(id_cols[i] == row, 1.0, seen)
        again = jnp.max(seen, axis=0, keepdims=True) > 0.0
        firsts = jnp.where(again, -1.0, row)
        first_rows[j : j + 1, :] = firsts
        first_cols[j] = columns_of(firsts)
    owner = jnp.floor((ids + 0.5) * (1.0 / VOCAB_ROWS))
    base = owner * float(VOCAB_ROWS)
    local_row = ids - base
    total_hi = jnp.zeros((8, 128), F32)
    total_lo = jnp.zeros((8, 128), F32)
    for j in range(blocks):
        row = ids[j : j + 1, :]
        low = base[j : j + 1, :]
        count = jnp.zeros((128, 128), F32)
        for i in range(blocks):
            other = first_cols[i]
            count = jnp.where((other >= low) & (other < row), count + 1.0, count)
        rank = jnp.sum(count, axis=0, keepdims=True).astype(I32)
        owner_j = owner[j : j + 1, :].astype(I32)
        slot_ref[j : j + 1, :] = owner_j * CAP + rank
        relative = (owner_j ^ me) * CAP + rank
        is_first = first_rows[j : j + 1, :] >= 0.0
        local_j = local_row[j : j + 1, :].astype(I32)
        high = jnp.where(is_first, local_j >> 4, 0).astype(F32)
        lows = jnp.where(is_first, (local_j & 15) + 1, 0).astype(F32)
        left = jnp.where((relative >> 7) == iota((8, 128), 0), 1.0, 0.0).astype(BF16)
        here = (relative & 127) == iota((128, 128), 0)
        nt = (((1,), (1,)), ((), ()))
        total_hi += lax.dot_general(
            left, jnp.where(here, high, 0.0).astype(BF16), nt, preferred_element_type=F32
        )
        total_lo += lax.dot_general(
            left, jnp.where(here, lows, 0.0).astype(BF16), nt, preferred_element_type=F32
        )
    want_ref[...] = (total_hi * 16.0 + total_lo).astype(I32) - 1


def wanted_rows(me, want):
    pieces = []
    slots = 8 * 128
    position = iota((slots, 128), 0) ^ (me * CAP)
    want_f = want.astype(F32)
    spread = jnp.zeros((slots, 128), F32)
    for r in range(8):
        spread = jnp.where((position >> 7) == r, want_f[r : r + 1, :], spread)
    mine = jnp.where((position & 127) == iota((slots, 128), 1), spread, 0.0)
    del pieces
    return jnp.sum(mine, axis=1, keepdims=True).astype(I32)


def fetch_rows(me_ref, want_ref, table_ref, rows_ref):
    wanted = wanted_rows(me_ref[0], want_ref[...])
    slots, owned = wanted.shape[0], table_ref.shape[1]
    pick = jnp.where(wanted == iota((slots, owned), 1), 1.0, 0.0).astype(BF16)
    rows_ref[...] = lax.dot_general(
        pick, table_ref[...], (((1,), (1,)), ((), ())), preferred_element_type=F32
    ).astype(BF16)


def sum_slots(cols_ref, slot_ref, rows_ref, out_ref, columns):
    blocks = cols_ref.shape[0]
    slots = rows_ref.shape[0]
    for u in range(blocks):
        tail = cols_ref[u, 128:192, :]
        columns[128 * u : 128 * u + 128, 0:128] = cols_ref[u, 0:128, :]
        columns[128 * u : 128 * u + 128, 128:192] = jnp.concatenate(
            [tail[:, 0:64], tail[:, 64:128]], axis=0
        )
    member = jnp.concatenate(
        [
            jnp.where(slot_ref[u : u + 1, :] == iota((slots, 128), 0), 1.0, 0.0).astype(BF16)
            for u in range(blocks)
        ],
        axis=1,
    )
    grads = jnp.dot(member, columns[...], preferred_element_type=F32).astype(BF16)
    owners = slots // CAP
    rows = rows_ref[...]
    out_ref[:, 0:16, :] = rows[:, 0:128].reshape(owners, CAP, 128)
    out_ref[:, 16:32, :] = grads[:, 0:128].reshape(owners, CAP, 128)
    out_ref[:, 32:48, :] = jnp.concatenate([rows[:, 128:192], grads[:, 128:192]], axis=1).reshape(
        owners, CAP, 128
    )


def spread_tokens(got_ref, slot_ref, out_ref):
    blocks = slot_ref.shape[0]
    owners = got_ref.shape[0]
    slots = owners * CAP
    normalizer = math.sqrt(D)
    main = got_ref[:, 0:16, :].reshape(slots, 128)
    tail = got_ref[:, 32:48, :].reshape(slots, 128)[:, 0:64]
    rows = jnp.concatenate([main, tail], axis=1)
    slot_f = slot_ref[...].astype(F32)
    for u in range(blocks):
        mine = columns_of(slot_f[u : u + 1, :])
        pick = jnp.concatenate(
            [
                jnp.where(mine == (iota((128, 128), 1) + 128 * k).astype(F32), 1.0, 0.0).astype(BF16)
                for k in range(slots // 128)
            ],
            axis=1,
        )
        tokens = (jnp.dot(pick, rows, preferred_element_type=F32) * normalizer).astype(BF16)
        out_ref[u, 0:128, :] = tokens[:, 0:128]
        out_ref[u, 128:192, :] = jnp.concatenate(
            [tokens[0:64, 128:192], tokens[64:128, 128:192]], axis=1
        )


def update_rows(me_ref, want_ref, got_ref, table_ref, moment_ref, new_table_ref, new_moment_ref):
    normalizer = math.sqrt(D)
    wanted = wanted_rows(me_ref[0], want_ref[...])
    slots, owned = wanted.shape[0], table_ref.shape[1]
    pick = jnp.where(wanted == iota((slots, owned), 1), 1.0, 0.0).astype(BF16)
    main = got_ref[:, 16:32, :].reshape(slots, 128)
    tail = got_ref[:, 32:48, :].reshape(slots, 128)
    tn = (((0,), (0,)), ((), ()))
    ones = jnp.ones((8, slots), BF16)
    hits = jnp.dot(ones, pick, preferred_element_type=F32)
    touched = hits[0:1, :] > 0.0
    sum_main = lax.dot_general(main, pick, tn, preferred_element_type=F32)
    sum_tail = lax.dot_general(tail, pick, tn, preferred_element_type=F32)[64:128, :]
    for lo, hi, summed in ((0, 128, sum_main), (128, 192, sum_tail)):
        gradient = summed * normalizer
        old_table = table_ref[lo:hi, :]
        old_moment = moment_ref[lo:hi, :]
        weights = old_table.astype(F32)
        moment_new = beta_two * old_moment.astype(F32) + (1.0 - beta_two) * gradient * gradient
        denominator = jnp.sqrt(moment_new / (1.0 - beta_two**STEP)) + epsilon
        updated = weights - learn_rate * (gradient / denominator + weight_decay * weights)
        new_table_ref[lo:hi, :] = jnp.where(touched, updated, weights).astype(BF16)
        new_moment_ref[lo:hi, :] = jnp.where(
            touched, moment_new, old_moment.astype(F32)
        ).astype(BF16)


def exchange_requests(want, dp_count):
    position = iota((8, 128), 0) * 8 + iota((8, 128), 1) // CAP
    bit = 1
    while bit < dp_count:
        pairs = [(g, g ^ bit) for g in range(dp_count)]
        got = lax.ppermute(want, "dp", pairs)
        want = jnp.where((position & bit) != 0, got, want)
        bit *= 2
    return want


def local(token_ids, embed_table, second_moment, cotangent):
    dp_count = lax.axis_size("dp")
    seq_count = lax.axis_size("seq")
    blocks = token_ids.shape[0] // 128
    slots = dp_count * CAP
    owned = embed_table.shape[0]
    S = jax.ShapeDtypeStruct
    me = lax.axis_index("dp").astype(I32).reshape(1)
    table = embed_table.T
    moment = second_moment.T
    ids = token_ids.reshape(blocks, 128)

    packed = call(pack_cotangent, S((seq_count, 192, 128), BF16), 1, nbytes=1200000)(cotangent)
    columns = lax.all_to_all(packed, "seq", split_axis=0, concat_axis=0, tiled=True)
    slot, want = call(
        number_slots,
        (S((blocks, 128), I32), S((8, 128), I32)),
        2,
        scratch=[
            pltpu.VMEM((blocks, 128, 128), F32),
            pltpu.VMEM((blocks, 128, 128), F32),
            pltpu.VMEM((16, 128), F32),
        ],
        smem_in=(0,),
        flops=10**6,
        nbytes=10**6,
    )(me, ids)
    want = exchange_requests(want, dp_count)
    rows = call(
        fetch_rows, S((slots, 192), BF16), 3, smem_in=(0,), flops=2 * slots * owned * 192, nbytes=1200000
    )(me, want, table)
    payload = call(
        sum_slots,
        S((dp_count, 48, 128), BF16),
        3,
        scratch=[pltpu.VMEM((blocks * 128, 192), BF16)],
        flops=2 * slots * blocks * 128 * 192,
        nbytes=1800000,
    )(columns, slot, rows)
    got = lax.all_to_all(payload, "dp", split_axis=0, concat_axis=0, tiled=True)
    tokens = call(
        spread_tokens, S((seq_count, 192, 128), BF16), 2, flops=2 * slots * blocks * 128 * 192, nbytes=1400000
    )(got, slot)
    arrived = lax.all_to_all(tokens, "seq", split_axis=0, concat_axis=0, tiled=True)
    new_table, new_moment = call(
        update_rows,
        (S((192, owned), BF16), S((192, owned), BF16)),
        5,
        smem_in=(0,),
        flops=2 * slots * owned * 192,
        nbytes=4000000,
    )(me, want, got, table, moment)
    embedded = call(unpack_tokens, S((128, seq_count * 192), BF16), 1, nbytes=1200000)(arrived)
    return embedded, new_table.T, new_moment.T


def solution(mesh):
    in_specs = (P("dp"), P("dp", "seq"), P("dp", "seq"), P(("dp", "seq"), None))
    out_specs = (P(("dp", "seq"), None), P("dp", "seq"), P("dp", "seq"))
    return jax.shard_map(local, mesh=mesh, in_specs=in_specs, out_specs=out_specs, check_vma=False)
```

time: 189 us -> 133 us (0.70)
  the two profiles are of different devices: /device:TPU:1 before, /device:TPU:71 now
where the time goes in v1:
time: 133 us
  starting transfers between devices  46.5 us (35%)
  blocking collectives  38.9 us (29%)
  waiting for transfers between devices  30.6 us (23%)
  Pallas kernels  13.7 us (10%)
  local copies, waits for them, and re-layouts  1.75 us (1%)
    all_to_all x1, blocking collectives, local(): got = lax.all_to_all(payload, 'dp', split_axis=0, concat_axis=0, tiled=True)  38.9 us
    ppermute x6, starting transfers between devices, exchange_requests(): got = lax.ppermute(want, 'dp', pairs)  22.9 us
    all_to_all x1, waiting for transfers between devices, local(): lax.all_to_all(tokens, 'seq', split_axis=0, concat_axis=0, tiled=True)  22.4 us
    all_to_all x1, starting transfers between devices, local(): lax.all_to_all(packed, 'seq', split_axis=0, concat_axis=0, tiled=True)  14.3 us
    all_to_all x1, starting transfers between devices, local(): lax.all_to_all(tokens, 'seq', split_axis=0, concat_axis=0, tiled=True)  9.19 us
    ppermute x6, waiting for transfers between devices, exchange_requests(): got = lax.ppermute(want, 'dp', pairs)  8.14 us
    pallas_call x1, Pallas kernels, local(): call(update_rows, (S((192, owned), BF16), S((192, owned), BF16)), 5, smem...  4.41 us
  transfers between devices with their start and end apart: 8, of which 6 were waited for; matrix products, arithmetic and copies ran while one was open for 0% of the time, Pallas kernels for 5%

profile of v1, /device:TPU:71, one launch (start us, length us, event | category | flops | bytes accessed | tf_op | source)
XLA Modules:
  0.0 132.6 jit_solution(1650168391931709896)
XLA Ops:
  0.6 0.0 copy-start.1
  0.6 0.7 copy-done.1
  1.3 2.3 %shard_map.68 = (s32[12,128]{1,0:T(8,128)S(1)}, s32[8,128]{1,0:T(8,128)S(1)}) custom-call(s32[1]{0:T(128)} %bitcast.me_ref, s32[12,128]{1,0:T(8,128)S(1)} %bitcast.6), custom_call_target="tpu_custom_call" | custom-call | flops 1000000 | bytes 1000000 | tf_op jit(solution)/shard_map/pallas_call | solution.py:244
  3.6 2.6 %collective-permute-start = (s32[8,128]{1,0:T(8,128)S(1)}, s32[8,128]{1,0:T(8,128)S(1)}, u32[]{:S(2)}, u32[]{:S(2)}) collective-permute-start(s32[8,128]{1,0:T(8,128)S(1)} %get-tuple-element.8), channel_id=1, source_target_pairs={{0,12},{12,0},{24,36},{36,24},{48,60},{60,48},{72,84},{84,72},{96,... | collective-permute-start | bytes 12296 | tf_op jit(solution)/shard_map/ppermute | solution.py:224
  6.3 0.0 copy-start
  6.3 1.1 copy-done
  7.3 1.0 shard_map.67
  8.4 0.0 copy-start.2
  8.4 14.3 %all-to-all-start = ((bf16[12,192,128]{2,1,0:T(8,128)(2,1)}), bf16[12,192,128]{2,1,0:T(8,128)(2,1)S(1)}, u32[]{:S(2)}, u32[]{:S(2)}) async-start(bf16[12,192,128]{2,1,0:T(8,128)(2,1)} %shard_map.67), calls=%async_computation | async-start | bytes 1179648 | tf_op jit(solution)/shard_map/all_to_all | solution.py:243
  22.7 0.0 collective-permute-done
  22.8 0.1 fusion.5
  22.8 3.2 %collective-permute-start.1 = (s32[8,128]{1,0:T(8,128)S(1)}, s32[8,128]{1,0:T(8,128)S(1)}, u32[]{:S(2)}, u32[]{:S(2)}) collective-permute-start(s32[8,128]{1,0:T(8,128)S(1)} %fusion.5), channel_id=1, source_target_pairs={{0,24},{12,36},{24,0},{36,12},{48,72},{60,84},{72,48},{84,60},{96,... | collective-permute-start | bytes 12296 | tf_op jit(solution)/shard_map/ppermute | solution.py:224
  26.0 1.1 collective-permute-done.1
  27.2 0.1 fusion.4
  27.2 4.2 %collective-permute-start.2 = (s32[8,128]{1,0:T(8,128)S(1)}, s32[8,128]{1,0:T(8,128)S(1)}, u32[]{:S(2)}, u32[]{:S(2)}) collective-permute-start(s32[8,128]{1,0:T(8,128)S(1)} %fusion.4), channel_id=1, source_target_pairs={{0,48},{12,60},{24,72},{36,84},{48,0},{60,12},{72,24},{84,36},{96,... | collective-permute-start | bytes 12296 | tf_op jit(solution)/shard_map/ppermute | solution.py:224
  31.5 1.3 collective-permute-done.2
  32.8 0.1 fusion.3
  32.9 7.4 %collective-permute-start.3 = (s32[8,128]{1,0:T(8,128)S(1)}, s32[8,128]{1,0:T(8,128)S(1)}, u32[]{:S(2)}, u32[]{:S(2)}) collective-permute-start(s32[8,128]{1,0:T(8,128)S(1)} %fusion.3), channel_id=1, source_target_pairs={{0,96},{12,108},{24,120},{36,132},{48,144},{60,156},{72,168},{84,1... | collective-permute-start | bytes 12296 | tf_op jit(solution)/shard_map/ppermute | solution.py:224
  40.3 1.0 collective-permute-done.3
  41.3 0.1 fusion.2
  41.4 2.4 %collective-permute-start.4 = (s32[8,128]{1,0:T(8,128)S(1)}, s32[8,128]{1,0:T(8,128)S(1)}, u32[]{:S(2)}, u32[]{:S(2)}) collective-permute-start(s32[8,128]{1,0:T(8,128)S(1)} %fusion.2), channel_id=1, source_target_pairs={{0,192},{12,204},{24,216},{36,228},{48,240},{60,252},{72,264},{84,... | collective-permute-start | bytes 12296 | tf_op jit(solution)/shard_map/ppermute | solution.py:224
  43.8 1.9 %collective-permute-done.4 = s32[8,128]{1,0:T(8,128)S(1)} collective-permute-done((s32[8,128]{1,0:T(8,128)S(1)}, s32[8,128]{1,0:T(8,128)S(1)}, u32[]{:S(2)}, u32[]{:S(2)}) %collective-permute-start.4) | collective-permute-done | bytes 4128 | tf_op jit(solution)/shard_map/ppermute | solution.py:224
  45.7 0.1 fusion.1
  45.8 3.0 %collective-permute-start.5 = (s32[8,128]{1,0:T(8,128)S(1)}, s32[8,128]{1,0:T(8,128)S(1)}, u32[]{:S(2)}, u32[]{:S(2)}) collective-permute-start(s32[8,128]{1,0:T(8,128)S(1)} %fusion.1), channel_id=1, source_target_pairs={{0,384},{12,396},{24,408},{36,420},{48,432},{60,444},{72,456},{84,... | collective-permute-start | bytes 12296 | tf_op jit(solution)/shard_map/ppermute | solution.py:224
  48.8 2.8 %collective-permute-done.5 = s32[8,128]{1,0:T(8,128)S(1)} collective-permute-done((s32[8,128]{1,0:T(8,128)S(1)}, s32[8,128]{1,0:T(8,128)S(1)}, u32[]{:S(2)}, u32[]{:S(2)}) %collective-permute-start.5) | collective-permute-done | bytes 4128 | tf_op jit(solution)/shard_map/ppermute | solution.py:224
  51.6 0.1 fusion.want_ref
  51.7 0.0 copy-done.2
  51.7 1.5 %shard_map.69.rows_ref = bf16[1024,192]{1,0:T(8,128)(2,1)S(1)} custom-call(s32[1]{0:T(128)} %bitcast.me_ref, s32[8,128]{1,0:T(8,128)S(1)} %fusion.want_ref, bf16[192,2000]{1,0:T(8,128)(2,1)S(1)} %bitcast.7), custom_call_target="tpu_custom_call" | custom-call | flops 786432000 | bytes 1200000 | tf_op jit(solution)/shard_map/pallas_call | solution.py:258
  53.2 0.0 all-to-all-done.cols_ref
  53.2 1.2 shard_map.70
  54.4 38.9 %all_to_all.15.got_ref = bf16[64,48,128]{2,1,0:T(8,128)(2,1)S(1)} all-to-all(bf16[64,48,128]{2,1,0:T(8,128)(2,1)S(1)} %shard_map.70), channel_id=1, replica_groups=mesh['dp'=64,'seq'=12] {'dp'}, dimensions={0} | all-to-all | bytes 1572864 | tf_op jit(solution)/shard_map/all_to_all | solution.py:269
  93.3 1.9 %shard_map.71 = bf16[12,192,128]{2,1,0:T(8,128)(2,1)} custom-call(bf16[64,48,128]{2,1,0:T(8,128)(2,1)S(1)} %all_to_all.15.got_ref, s32[12,128]{1,0:T(8,128)S(1)} %get-tuple-element.7.slot_ref), custom_call_target="tpu_custom_call" | custom-call | flops 603979776 | bytes 1400000 | tf_op jit(solution)/shard_map/pallas_call | solution.py:270
  95.2 0.0 copy-start.3
  95.2 9.2 %all-to-all-start.2 = ((bf16[12,192,128]{2,1,0:T(8,128)(2,1)}), bf16[12,192,128]{2,1,0:T(8,128)(2,1)S(1)}, u32[]{:S(2)}, u32[]{:S(2)}) async-start(bf16[12,192,128]{2,1,0:T(8,128)(2,1)} %shard_map.71), calls=%async_computation.2 | async-start | bytes 1179648 | tf_op jit(solution)/shard_map/all_to_all | solution.py:273
  104.4 0.0 copy-done.3
  104.4 4.4 %shard_map.73 = (bf16[192,2000]{1,0:T(8,128)(2,1)}, bf16[192,2000]{1,0:T(8,128)(2,1)}) custom-call(s32[1]{0:T(128)} %bitcast.me_ref, s32[8,128]{1,0:T(8,128)S(1)} %fusion.want_ref, bf16[64,48,128]{2,1,0:T(8,128)(2,1)S(1)} %all_to_all.15.got_ref, bf16[192,2000]{1,0:T(8,128)(2,1)S(1)} %bitcast.8, bf16[192,2000]{1,0:T(8,128)(2,1)S(1)} %bitcast.9), custom_call_target="tpu_custom_call" | custom-call | flops 786432000 | bytes 4000000 | tf_op jit(solution)/shard_map/pallas_call | solution.py:274
  108.8 22.4 %all-to-all-done.2.in_ref = bf16[12,192,128]{2,1,0:T(8,128)(2,1)S(1)} async-done(((bf16[12,192,128]{2,1,0:T(8,128)(2,1)}), bf16[12,192,128]{2,1,0:T(8,128)(2,1)S(1)}, u32[]{:S(2)}, u32[]{:S(2)}) %all-to-all-start.2) | async-done | bytes 589856 | tf_op jit(solution)/shard_map/all_to_all | solution.py:273
  131.2 1.3 %shard_map.72 = bf16[128,2304]{1,0:T(8,128)(2,1)} custom-call(bf16[12,192,128]{2,1,0:T(8,128)(2,1)S(1)} %all-to-all-done.2.in_ref), custom_call_target="tpu_custom_call" | custom-call | bytes 1200000 | tf_op jit(solution)/shard_map/pallas_call | solution.py:282
  (3 shorter events, 0.0 us)
Async XLA Ops:
  0.6 0.7 copy-start.1
  3.6 19.1 %collective-permute-start = (s32[8,128]{1,0:T(8,128)S(1)}, s32[8,128]{1,0:T(8,128)S(1)}, u32[]{:S(2)}, u32[]{:S(2)}) collective-permute-start(s32[8,128]{1,0:T(8,128)S(1)} %get-tuple-element.8), channel_id=1, source_target_pairs={{0,12},{12,0},{24,36},{36,24},{48,60},{60,48},{72,84},{84,72},{96,... | collective-permute-start | bytes 12296 | tf_op jit(solution)/shard_map/ppermute | solution.py:224
  6.3 1.1 copy-start
  8.4 43.3 %copy-start.2 = (bf16[2000,192]{0,1:T(8,128)(2,1)S(1)}, bf16[2000,192]{0,1:T(8,128)(2,1)}, u32[]{:S(2)}) copy-start(bf16[2000,192]{0,1:T(8,128)(2,1)} %param.5) | copy-start | bytes 2304004
  8.4 44.8 %all-to-all-start = ((bf16[12,192,128]{2,1,0:T(8,128)(2,1)}), bf16[12,192,128]{2,1,0:T(8,128)(2,1)S(1)}, u32[]{:S(2)}, u32[]{:S(2)}) async-start(bf16[12,192,128]{2,1,0:T(8,128)(2,1)} %shard_map.67), calls=%async_computation | async-start | bytes 1179648 | tf_op jit(solution)/shard_map/all_to_all | solution.py:243
  22.8 4.3 %collective-permute-start.1 = (s32[8,128]{1,0:T(8,128)S(1)}, s32[8,128]{1,0:T(8,128)S(1)}, u32[]{:S(2)}, u32[]{:S(2)}) collective-permute-start(s32[8,128]{1,0:T(8,128)S(1)} %fusion.5), channel_id=1, source_target_pairs={{0,24},{12,36},{24,0},{36,12},{48,72},{60,84},{72,48},{84,60},{96,... | collective-permute-start | bytes 12296 | tf_op jit(solution)/shard_map/ppermute | solution.py:224
  27.2 5.5 %collective-permute-start.2 = (s32[8,128]{1,0:T(8,128)S(1)}, s32[8,128]{1,0:T(8,128)S(1)}, u32[]{:S(2)}, u32[]{:S(2)}) collective-permute-start(s32[8,128]{1,0:T(8,128)S(1)} %fusion.4), channel_id=1, source_target_pairs={{0,48},{12,60},{24,72},{36,84},{48,0},{60,12},{72,24},{84,36},{96,... | collective-permute-start | bytes 12296 | tf_op jit(solution)/shard_map/ppermute | solution.py:224
  32.9 8.4 %collective-permute-start.3 = (s32[8,128]{1,0:T(8,128)S(1)}, s32[8,128]{1,0:T(8,128)S(1)}, u32[]{:S(2)}, u32[]{:S(2)}) collective-permute-start(s32[8,128]{1,0:T(8,128)S(1)} %fusion.3), channel_id=1, source_target_pairs={{0,96},{12,108},{24,120},{36,132},{48,144},{60,156},{72,168},{84,1... | collective-permute-start | bytes 12296 | tf_op jit(solution)/shard_map/ppermute | solution.py:224
  41.4 4.3 %collective-permute-start.4 = (s32[8,128]{1,0:T(8,128)S(1)}, s32[8,128]{1,0:T(8,128)S(1)}, u32[]{:S(2)}, u32[]{:S(2)}) collective-permute-start(s32[8,128]{1,0:T(8,128)S(1)} %fusion.2), channel_id=1, source_target_pairs={{0,192},{12,204},{24,216},{36,228},{48,240},{60,252},{72,264},{84,... | collective-permute-start | bytes 12296 | tf_op jit(solution)/shard_map/ppermute | solution.py:224
  45.8 5.8 %collective-permute-start.5 = (s32[8,128]{1,0:T(8,128)S(1)}, s32[8,128]{1,0:T(8,128)S(1)}, u32[]{:S(2)}, u32[]{:S(2)}) collective-permute-start(s32[8,128]{1,0:T(8,128)S(1)} %fusion.1), channel_id=1, source_target_pairs={{0,384},{12,396},{24,408},{36,420},{48,432},{60,444},{72,456},{84,... | collective-permute-start | bytes 12296 | tf_op jit(solution)/shard_map/ppermute | solution.py:224
  95.2 9.2 %copy-start.3 = (bf16[2000,192]{0,1:T(8,128)(2,1)S(1)}, bf16[2000,192]{0,1:T(8,128)(2,1)}, u32[]{:S(2)}) copy-start(bf16[2000,192]{0,1:T(8,128)(2,1)} %param.6) | copy-start | bytes 2304004
  95.2 36.0 %all-to-all-start.2 = ((bf16[12,192,128]{2,1,0:T(8,128)(2,1)}), bf16[12,192,128]{2,1,0:T(8,128)(2,1)S(1)}, u32[]{:S(2)}, u32[]{:S(2)}) async-start(bf16[12,192,128]{2,1,0:T(8,128)(2,1)} %shard_map.71), calls=%async_computation.2 | async-start | bytes 1179648 | tf_op jit(solution)/shard_map/all_to_all | solution.py:273

commit v2 on v1

--- a/solution.py
+++ b/solution.py
@@ -17,6 +17,11 @@
 epsilon = 1e-08
 learn_rate = 0.01
 weight_decay = 0.1
+
+GRADS_ORDER = [(1 * k + 11) % 12 for k in range(12)]
+ROWS_ORDER = [(1 * k + 5) % 12 for k in range(12)]
+
+FLIP = 8
 
 BF16 = jnp.bfloat16
 F32 = jnp.float32
@@ -49,16 +54,18 @@
 def pack_cotangent(cot_ref, out_ref):
     for peer in range(out_ref.shape[0]):
         block = cot_ref[:, 192 * peer : 192 * peer + 192]
-        out_ref[peer, 0:128, :] = block[:, 0:128]
-        out_ref[peer, 128:192, :] = jnp.concatenate(
+        place = GRADS_ORDER.index(peer)
+        out_ref[place, 0:128, :] = block[:, 0:128]
+        out_ref[place, 128:192, :] = jnp.concatenate(
             [block[0:64, 128:192], block[64:128, 128:192]], axis=1
         )
 
 
 def unpack_tokens(in_ref, out_ref):
     for peer in range(in_ref.shape[0]):
-        tail = in_ref[peer, 128:192, :]
-        out_ref[:, 192 * peer : 192 * peer + 128] = in_ref[peer, 0:128, :]
+        place = ROWS_ORDER.index(peer)
+        tail = in_ref[place, 128:192, :]
+        out_ref[:, 192 * peer : 192 * peer + 128] = in_ref[place, 0:128, :]
         out_ref[:, 192 * peer + 128 : 192 * peer + 192] = jnp.concatenate(
             [tail[:, 0:64], tail[:, 64:128]], axis=0
         )
@@ -70,7 +77,7 @@
 
 def number_slots(me_ref, ids_ref, slot_ref, want_ref, id_cols, first_cols, first_rows):
     blocks = ids_ref.shape[0]
-    me = me_ref[0]
+    me = me_ref[0] & 15
     ids = ids_ref[...].astype(F32)
     for i in range(blocks):
         id_cols[i] = columns_of(ids[i : i + 1, :])
@@ -98,7 +105,7 @@
             count = jnp.where((other >= low) & (other < row), count + 1.0, count)
         rank = jnp.sum(count, axis=0, keepdims=True).astype(I32)
         owner_j = owner[j : j + 1, :].astype(I32)
-        slot_ref[j : j + 1, :] = owner_j * CAP + rank
+        slot_ref[j : j + 1, :] = (owner_j ^ FLIP) * CAP + rank
         relative = (owner_j ^ me) * CAP + rank
         is_first = first_rows[j : j + 1, :] >= 0.0
         local_j = local_row[j : j + 1, :].astype(I32)
@@ -113,19 +120,19 @@
         total_lo += lax.dot_general(
             left, jnp.where(here, lows, 0.0).astype(BF16), nt, preferred_element_type=F32
         )
-    want_ref[...] = (total_hi * 16.0 + total_lo).astype(I32) - 1
+    want = (total_hi * 16.0 + total_lo).astype(I32) - 1
+    for x in range(4):
+        want_ref[x] = want[2 * x : 2 * x + 2, :]
 
 
 def wanted_rows(me, want):
-    pieces = []
     slots = 8 * 128
-    position = iota((slots, 128), 0) ^ (me * CAP)
+    position = iota((slots, 128), 0) ^ (((me & 15) ^ FLIP) * CAP)
     want_f = want.astype(F32)
     spread = jnp.zeros((slots, 128), F32)
     for r in range(8):
-        spread = jnp.where((position >> 7) == r, want_f[r : r + 1, :], spread)
+        spread = jnp.where((position >> 7) == r, want_f[r // 2, r % 2 : r % 2 + 1, :], spread)
     mine = jnp.where((position & 127) == iota((slots, 128), 1), spread, 0.0)
-    del pieces
     return jnp.sum(mine, axis=1, keepdims=True).astype(I32)
 
 
@@ -142,8 +149,9 @@
     blocks = cols_ref.shape[0]
     slots = rows_ref.shape[0]
     for u in range(blocks):
-        tail = cols_ref[u, 128:192, :]
-        columns[128 * u : 128 * u + 128, 0:128] = cols_ref[u, 0:128, :]
+        place = GRADS_ORDER.index(u)
+        tail = cols_ref[place, 128:192, :]
+        columns[128 * u : 128 * u + 128, 0:128] = cols_ref[place, 0:128, :]
         columns[128 * u : 128 * u + 128, 128:192] = jnp.concatenate(
             [tail[:, 0:64], tail[:, 64:128]], axis=0
         )
@@ -183,8 +191,9 @@
             axis=1,
         )
         tokens = (jnp.dot(pick, rows, preferred_element_type=F32) * normalizer).astype(BF16)
-        out_ref[u, 0:128, :] = tokens[:, 0:128]
-        out_ref[u, 128:192, :] = jnp.concatenate(
+        place = ROWS_ORDER.index(u)
+        out_ref[place, 0:128, :] = tokens[:, 0:128]
+        out_ref[place, 128:192, :] = jnp.concatenate(
             [tokens[0:64, 128:192], tokens[64:128, 128:192]], axis=1
         )
 
@@ -217,13 +226,14 @@
 
 
 def exchange_requests(want, dp_count):
-    position = iota((8, 128), 0) * 8 + iota((8, 128), 1) // CAP
-    bit = 1
-    while bit < dp_count:
-        pairs = [(g, g ^ bit) for g in range(dp_count)]
-        got = lax.ppermute(want, "dp", pairs)
+    across_x = [[x * 16 + rest for x in range(4)] for rest in range(16)]
+    want = lax.all_to_all(
+        want, "dp", split_axis=0, concat_axis=0, tiled=True, axis_index_groups=across_x
+    )
+    position = iota(want.shape, 1) * 8 + iota(want.shape, 2) // CAP
+    for bit in (1, 2, 4, 8):
+        got = lax.ppermute(want, "dp", [(g, g ^ bit) for g in range(dp_count)])
         want = jnp.where((position & bit) != 0, got, want)
-        bit *= 2
     return want
 
 
@@ -240,10 +250,12 @@
     ids = token_ids.reshape(blocks, 128)
 
     packed = call(pack_cotangent, S((seq_count, 192, 128), BF16), 1, nbytes=1200000)(cotangent)
-    columns = lax.all_to_all(packed, "seq", split_axis=0, concat_axis=0, tiled=True)
+    columns = lax.all_to_all(
+        packed, "seq", split_axis=0, concat_axis=0, tiled=True, axis_index_groups=[GRADS_ORDER]
+    )
     slot, want = call(
         number_slots,
-        (S((blocks, 128), I32), S((8, 128), I32)),
+        (S((blocks, 128), I32), S((4, 2, 128), I32)),
         2,
         scratch=[
             pltpu.VMEM((blocks, 128, 128), F32),
@@ -266,11 +278,16 @@
         flops=2 * slots * blocks * 128 * 192,
         nbytes=1800000,
     )(columns, slot, rows)
-    got = lax.all_to_all(payload, "dp", split_axis=0, concat_axis=0, tiled=True)
+    flipped = [[k ^ FLIP for k in range(dp_count)]]
+    got = lax.all_to_all(
+        payload, "dp", split_axis=0, concat_axis=0, tiled=True, axis_index_groups=flipped
+    )
     tokens = call(
         spread_tokens, S((seq_count, 192, 128), BF16), 2, flops=2 * slots * blocks * 128 * 192, nbytes=1400000
     )(got, slot)
-    arrived = lax.all_to_all(tokens, "seq", split_axis=0, concat_axis=0, tiled=True)
+    arrived = lax.all_to_all(
+        tokens, "seq", split_axis=0, concat_axis=0, tiled=True, axis_index_groups=[ROWS_ORDER]
+    )
     new_table, new_moment = call(
         update_rows,
         (S((192, owned), BF16), S((192, owned), BF16)),

time: 133 us -> 121 us (0.910)
  the two profiles are of different devices: /device:TPU:71 before, /device:TPU:1 now
where the time goes in v2:
time: 121 us; the launch traced here: 120 us
  starting transfers between devices  48.9 us (40%)
  blocking collectives  32 us (26%)
  waiting for transfers between devices  22.2 us (18%)
  Pallas kernels  14.3 us (12%)
  local copies, waits for them, and re-layouts  1.76 us (1%)
    all_to_all x1, blocking collectives, local(): lax.all_to_all(payload, 'dp', split_axis=0, concat_axis=0, tiled=True, ax...  32 us
    ppermute x4, starting transfers between devices, exchange_requests(): got = lax.ppermute(want, 'dp', [(g, g ^ bit) for g in range(dp_count)])  19.1 us
    all_to_all x1, starting transfers between devices, local(): lax.all_to_all(packed, 'seq', split_axis=0, concat_axis=0, tiled=True, ax...  15.9 us
    all_to_all x1, waiting for transfers between devices, local(): lax.all_to_all(tokens, 'seq', split_axis=0, concat_axis=0, tiled=True, ax...  15.3 us
    all_to_all x1, starting transfers between devices, local(): lax.all_to_all(tokens, 'seq', split_axis=0, concat_axis=0, tiled=True, ax...  9.05 us
    all_to_all x1, starting transfers between devices, exchange_requests(): lax.all_to_all(want, 'dp', split_axis=0, concat_axis=0, tiled=True, axis_...  4.84 us
    ppermute x4, waiting for transfers between devices, exchange_requests(): got = lax.ppermute(want, 'dp', [(g, g ^ bit) for g in range(dp_count)])  4.82 us
    pallas_call x1, Pallas kernels, local(): call(update_rows, (S((192, owned), BF16), S((192, owned), BF16)), 5, smem...  4.41 us
  transfers between devices with their start and end apart: 7, of which 6 were waited for; matrix products, arithmetic and copies ran while one was open for 0% of the time, Pallas kernels for 6%

profile of v2, /device:TPU:1, one launch (start us, length us, event | category | flops | bytes accessed | tf_op | source)
XLA Modules:
  0.0 120.2 jit_solution(17698310084030315989)
XLA Ops:
  0.6 0.0 copy-start.1
  0.6 0.7 copy-done.1
  1.3 2.9 %shard_map.68 = (s32[12,128]{1,0:T(8,128)S(1)}, s32[4,2,128]{2,1,0:T(2,128)}) custom-call(s32[1]{0:T(128)} %bitcast.me_ref, s32[12,128]{1,0:T(8,128)S(1)} %bitcast.6), custom_call_target="tpu_custom_call" | custom-call | flops 1000000 | bytes 1000000 | tf_op jit(solution)/shard_map/pallas_call | solution.py:256
  4.3 4.8 %all-to-all-start.1 = ((s32[4,2,128]{2,1,0:T(2,128)}), s32[4,2,128]{2,1,0:T(2,128)S(1)}, u32[]{:S(2)}, u32[]{:S(2)}) async-start(s32[4,2,128]{2,1,0:T(2,128)} %get-tuple-element.8), calls=%async_computation.1 | async-start | bytes 8192 | tf_op jit(solution)/shard_map/all_to_all | solution.py:230
  9.1 0.0 copy-start
  9.1 1.1 copy-done
  10.2 1.0 shard_map.67
  11.2 0.0 copy-start.2
  11.2 2.0 %all-to-all-done.1 = s32[4,2,128]{2,1,0:T(2,128)S(1)} async-done(((s32[4,2,128]{2,1,0:T(2,128)}), s32[4,2,128]{2,1,0:T(2,128)S(1)}, u32[]{:S(2)}, u32[]{:S(2)}) %all-to-all-start.1) | async-done | bytes 4128 | tf_op jit(solution)/shard_map/all_to_all | solution.py:230
  13.3 15.9 %all-to-all-start = ((bf16[12,192,128]{2,1,0:T(8,128)(2,1)}), bf16[12,192,128]{2,1,0:T(8,128)(2,1)S(1)}, u32[]{:S(2)}, u32[]{:S(2)}) async-start(bf16[12,192,128]{2,1,0:T(8,128)(2,1)} %shard_map.67), calls=%async_computation | async-start | bytes 1179648 | tf_op jit(solution)/shard_map/all_to_all | solution.py:253
  29.1 4.3 %collective-permute-start = (s32[4,2,128]{2,1,0:T(2,128)S(1)}, s32[4,2,128]{2,1,0:T(2,128)S(1)}, u32[]{:S(2)}, u32[]{:S(2)}) collective-permute-start(s32[4,2,128]{2,1,0:T(2,128)S(1)} %all-to-all-done.1), channel_id=1, source_target_pairs={{0,12},{12,0},{24,36},{36,24},{48,60},{60,48},{72,84},{84,72},{96,... | collective-permute-start | bytes 12296 | tf_op jit(solution)/shard_map/ppermute | solution.py:235
  33.5 0.8 collective-permute-done
  34.2 0.1 compare_select_fusion
  34.3 3.2 %collective-permute-start.1 = (s32[4,2,128]{2,1,0:T(2,128)S(1)}, s32[4,2,128]{2,1,0:T(2,128)S(1)}, u32[]{:S(2)}, u32[]{:S(2)}) collective-permute-start(s32[4,2,128]{2,1,0:T(2,128)S(1)} %compare_select_fusion), channel_id=1, source_target_pairs={{0,24},{12,36},{24,0},{36,12},{48,72},{60,84},{72,48},{84,60},{96,... | collective-permute-start | bytes 12296 | tf_op jit(solution)/shard_map/ppermute | solution.py:235
  37.5 1.4 %collective-permute-done.1 = s32[4,2,128]{2,1,0:T(2,128)S(1)} collective-permute-done((s32[4,2,128]{2,1,0:T(2,128)S(1)}, s32[4,2,128]{2,1,0:T(2,128)S(1)}, u32[]{:S(2)}, u32[]{:S(2)}) %collective-permute-start.1) | collective-permute-done | bytes 4128 | tf_op jit(solution)/shard_map/ppermute | solution.py:235
  38.9 0.1 compare_select_fusion.1
  39.0 4.2 %collective-permute-start.2 = (s32[4,2,128]{2,1,0:T(2,128)S(1)}, s32[4,2,128]{2,1,0:T(2,128)S(1)}, u32[]{:S(2)}, u32[]{:S(2)}) collective-permute-start(s32[4,2,128]{2,1,0:T(2,128)S(1)} %compare_select_fusion.1), channel_id=1, source_target_pairs={{0,48},{12,60},{24,72},{36,84},{48,0},{60,12},{72,24},{84,36},{96,... | collective-permute-start | bytes 12296 | tf_op jit(solution)/shard_map/ppermute | solution.py:235
  43.2 1.3 %collective-permute-done.2 = s32[4,2,128]{2,1,0:T(2,128)S(1)} collective-permute-done((s32[4,2,128]{2,1,0:T(2,128)S(1)}, s32[4,2,128]{2,1,0:T(2,128)S(1)}, u32[]{:S(2)}, u32[]{:S(2)}) %collective-permute-start.2) | collective-permute-done | bytes 4128 | tf_op jit(solution)/shard_map/ppermute | solution.py:235
  44.6 0.1 compare_select_fusion.2
  44.6 7.4 %collective-permute-start.3 = (s32[4,2,128]{2,1,0:T(2,128)S(1)}, s32[4,2,128]{2,1,0:T(2,128)S(1)}, u32[]{:S(2)}, u32[]{:S(2)}) collective-permute-start(s32[4,2,128]{2,1,0:T(2,128)S(1)} %compare_select_fusion.2), channel_id=1, source_target_pairs={{0,96},{12,108},{24,120},{36,132},{48,144},{60,156},{72,168},{84,1... | collective-permute-start | bytes 12296 | tf_op jit(solution)/shard_map/ppermute | solution.py:235
  52.1 1.3 %collective-permute-done.3 = s32[4,2,128]{2,1,0:T(2,128)S(1)} collective-permute-done((s32[4,2,128]{2,1,0:T(2,128)S(1)}, s32[4,2,128]{2,1,0:T(2,128)S(1)}, u32[]{:S(2)}, u32[]{:S(2)}) %collective-permute-start.3) | collective-permute-done | bytes 4128 | tf_op jit(solution)/shard_map/ppermute | solution.py:235
  53.4 0.1 compare_select_fusion.3.want_ref
  53.4 0.0 copy-done.2
  53.4 1.5 %shard_map.69.rows_ref = bf16[1024,192]{1,0:T(8,128)(2,1)S(1)} custom-call(s32[1]{0:T(128)} %bitcast.me_ref, s32[4,2,128]{2,1,0:T(2,128)S(1)} %compare_select_fusion.3.want_ref, bf16[192,2000]{1,0:T(8,128)(2,1)S(1)} %bitcast.7), custom_call_target="tpu_custom_call" | custom-call | flops 786432000 | bytes 1200000 | tf_op jit(solution)/shard_map/pallas_call | solution.py:270
  55.0 0.0 all-to-all-done.cols_ref
  55.0 1.2 shard_map.70
  56.1 32.0 %all_to_all.20.got_ref = bf16[64,48,128]{2,1,0:T(8,128)(2,1)S(1)} all-to-all(bf16[64,48,128]{2,1,0:T(8,128)(2,1)S(1)} %shard_map.70), channel_id=1, replica_groups={{96,108,120,132,144,156,168,180,0,12,24,36,48,60,72,84,288,300,312,324,..., dimensions={0} | all-to-all | bytes 1572864 | tf_op jit(solution)/shard_map/all_to_all | solution.py:282
  88.1 1.9 %shard_map.71 = bf16[12,192,128]{2,1,0:T(8,128)(2,1)} custom-call(bf16[64,48,128]{2,1,0:T(8,128)(2,1)S(1)} %all_to_all.20.got_ref, s32[12,128]{1,0:T(8,128)S(1)} %get-tuple-element.7.slot_ref), custom_call_target="tpu_custom_call" | custom-call | flops 603979776 | bytes 1400000 | tf_op jit(solution)/shard_map/pallas_call | solution.py:285
  90.0 0.0 copy-start.3
  90.0 9.0 %all-to-all-start.3 = ((bf16[12,192,128]{2,1,0:T(8,128)(2,1)}), bf16[12,192,128]{2,1,0:T(8,128)(2,1)S(1)}, u32[]{:S(2)}, u32[]{:S(2)}) async-start(bf16[12,192,128]{2,1,0:T(8,128)(2,1)} %shard_map.71), calls=%async_computation.3 | async-start | bytes 1179648 | tf_op jit(solution)/shard_map/all_to_all | solution.py:288
  99.1 0.0 copy-done.3
  99.1 4.4 %shard_map.73 = (bf16[192,2000]{1,0:T(8,128)(2,1)}, bf16[192,2000]{1,0:T(8,128)(2,1)}) custom-call(s32[1]{0:T(128)} %bitcast.me_ref, s32[4,2,128]{2,1,0:T(2,128)S(1)} %compare_select_fusion.3.want_ref, bf16[64,48,128]{2,1,0:T(8,128)(2,1)S(1)} %all_to_all.20.got_ref, bf16[192,2000]{1,0:T(8,128)(2,1)S(1)} %bitcast.8, bf16[192,2000]{1,0:T(8,128)(2,1)S(1)} %bitcast.9), custom_call_target="tpu_custom_call" | custom-call | flops 786432000 | bytes 4000000 | tf_op jit(solution)/shard_map/pallas_call | solution.py:291
  103.5 15.3 %all-to-all-done.3.in_ref = bf16[12,192,128]{2,1,0:T(8,128)(2,1)S(1)} async-done(((bf16[12,192,128]{2,1,0:T(8,128)(2,1)}), bf16[12,192,128]{2,1,0:T(8,128)(2,1)S(1)}, u32[]{:S(2)}, u32[]{:S(2)}) %all-to-all-start.3) | async-done | bytes 589856 | tf_op jit(solution)/shard_map/all_to_all | solution.py:288
  118.8 1.3 %shard_map.72 = bf16[128,2304]{1,0:T(8,128)(2,1)} custom-call(bf16[12,192,128]{2,1,0:T(8,128)(2,1)S(1)} %all-to-all-done.3.in_ref), custom_call_target="tpu_custom_call" | custom-call | bytes 1200000 | tf_op jit(solution)/shard_map/pallas_call | solution.py:299
  (4 shorter events, 0.0 us)
Async XLA Ops:
  0.6 0.7 copy-start.1
  4.3 9.0 %all-to-all-start.1 = ((s32[4,2,128]{2,1,0:T(2,128)}), s32[4,2,128]{2,1,0:T(2,128)S(1)}, u32[]{:S(2)}, u32[]{:S(2)}) async-start(s32[4,2,128]{2,1,0:T(2,128)} %get-tuple-element.8), calls=%async_computation.1 | async-start | bytes 8192 | tf_op jit(solution)/shard_map/all_to_all | solution.py:230
  9.1 1.1 copy-start
  11.2 42.2 %copy-start.2 = (bf16[2000,192]{0,1:T(8,128)(2,1)S(1)}, bf16[2000,192]{0,1:T(8,128)(2,1)}, u32[]{:S(2)}) copy-start(bf16[2000,192]{0,1:T(8,128)(2,1)} %param.5) | copy-start | bytes 2304004
  13.3 41.7 %all-to-all-start = ((bf16[12,192,128]{2,1,0:T(8,128)(2,1)}), bf16[12,192,128]{2,1,0:T(8,128)(2,1)S(1)}, u32[]{:S(2)}, u32[]{:S(2)}) async-start(bf16[12,192,128]{2,1,0:T(8,128)(2,1)} %shard_map.67), calls=%async_computation | async-start | bytes 1179648 | tf_op jit(solution)/shard_map/all_to_all | solution.py:253
  29.1 5.1 %collective-permute-start = (s32[4,2,128]{2,1,0:T(2,128)S(1)}, s32[4,2,128]{2,1,0:T(2,128)S(1)}, u32[]{:S(2)}, u32[]{:S(2)}) collective-permute-start(s32[4,2,128]{2,1,0:T(2,128)S(1)} %all-to-all-done.1), channel_id=1, source_target_pairs={{0,12},{12,0},{24,36},{36,24},{48,60},{60,48},{72,84},{84,72},{96,... | collective-permute-start | bytes 12296 | tf_op jit(solution)/shard_map/ppermute | solution.py:235
  34.3 4.6 %collective-permute-start.1 = (s32[4,2,128]{2,1,0:T(2,128)S(1)}, s32[4,2,128]{2,1,0:T(2,128)S(1)}, u32[]{:S(2)}, u32[]{:S(2)}) collective-permute-start(s32[4,2,128]{2,1,0:T(2,128)S(1)} %compare_select_fusion), channel_id=1, source_target_pairs={{0,24},{12,36},{24,0},{36,12},{48,72},{60,84},{72,48},{84,60},{96,... | collective-permute-start | bytes 12296 | tf_op jit(solution)/shard_map/ppermute | solution.py:235
  39.0 5.5 %collective-permute-start.2 = (s32[4,2,128]{2,1,0:T(2,128)S(1)}, s32[4,2,128]{2,1,0:T(2,128)S(1)}, u32[]{:S(2)}, u32[]{:S(2)}) collective-permute-start(s32[4,2,128]{2,1,0:T(2,128)S(1)} %compare_select_fusion.1), channel_id=1, source_target_pairs={{0,48},{12,60},{24,72},{36,84},{48,0},{60,12},{72,24},{84,36},{96,... | collective-permute-start | bytes 12296 | tf_op jit(solution)/shard_map/ppermute | solution.py:235
  44.6 8.7 %collective-permute-start.3 = (s32[4,2,128]{2,1,0:T(2,128)S(1)}, s32[4,2,128]{2,1,0:T(2,128)S(1)}, u32[]{:S(2)}, u32[]{:S(2)}) collective-permute-start(s32[4,2,128]{2,1,0:T(2,128)S(1)} %compare_select_fusion.2), channel_id=1, source_target_pairs={{0,96},{12,108},{24,120},{36,132},{48,144},{60,156},{72,168},{84,1... | collective-permute-start | bytes 12296 | tf_op jit(solution)/shard_map/ppermute | solution.py:235
  90.0 9.1 %copy-start.3 = (bf16[2000,192]{0,1:T(8,128)(2,1)S(1)}, bf16[2000,192]{0,1:T(8,128)(2,1)}, u32[]{:S(2)}) copy-start(bf16[2000,192]{0,1:T(8,128)(2,1)} %param.6) | copy-start | bytes 2304004
  90.0 28.8 %all-to-all-start.3 = ((bf16[12,192,128]{2,1,0:T(8,128)(2,1)}), bf16[12,192,128]{2,1,0:T(8,128)(2,1)S(1)}, u32[]{:S(2)}, u32[]{:S(2)}) async-start(bf16[12,192,128]{2,1,0:T(8,128)(2,1)} %shard_map.71), calls=%async_computation.3 | async-start | bytes 1179648 | tf_op jit(solution)/shard_map/all_to_all | solution.py:288

commit v3 on v2

--- a/solution.py
+++ b/solution.py
@@ -29,7 +29,7 @@
 VMEM_LIMIT = 48 * 1024 * 1024
 
 
-def call(kernel, out_shape, n_in, scratch=(), smem_in=(), flops=0, nbytes=0):
+def call(kernel, out_shape, n_in, scratch=(), smem_in=(), out_space=pltpu.VMEM, flops=0, nbytes=0):
     def spec(i):
         return pl.BlockSpec(memory_space=pltpu.SMEM if i in smem_in else pltpu.VMEM)
 
@@ -38,9 +38,9 @@
         kernel,
         out_shape=out_shape,
         in_specs=[spec(i) for i in range(n_in)],
-        out_specs=[pl.BlockSpec(memory_space=pltpu.VMEM) for _ in out_shape]
+        out_specs=[pl.BlockSpec(memory_space=out_space) for _ in out_shape]
         if many
-        else pl.BlockSpec(memory_space=pltpu.VMEM),
+        else pl.BlockSpec(memory_space=out_space),
         scratch_shapes=list(scratch),
         compiler_params=pltpu.CompilerParams(vmem_limit_bytes=VMEM_LIMIT),
         cost_estimate=pl.CostEstimate(flops=flops, bytes_accessed=nbytes, transcendentals=0),
@@ -61,14 +61,23 @@
         )
 
 
-def unpack_tokens(in_ref, out_ref):
-    for peer in range(in_ref.shape[0]):
-        place = ROWS_ORDER.index(peer)
-        tail = in_ref[place, 128:192, :]
-        out_ref[:, 192 * peer : 192 * peer + 128] = in_ref[place, 0:128, :]
-        out_ref[:, 192 * peer + 128 : 192 * peer + 192] = jnp.concatenate(
-            [tail[:, 0:64], tail[:, 64:128]], axis=0
-        )
+def unpack_tokens(in_ref, out_ref, rows, sems):
+    copies = []
+    for pair in range(in_ref.shape[0] // 2):
+        for peer in (2 * pair, 2 * pair + 1):
+            place = ROWS_ORDER.index(peer)
+            tail = in_ref[place, 128:192, :]
+            rows[:, 192 * peer : 192 * peer + 128] = in_ref[place, 0:128, :]
+            rows[:, 192 * peer + 128 : 192 * peer + 192] = jnp.concatenate(
+                [tail[:, 0:64], tail[:, 64:128]], axis=0
+            )
+        columns = pl.ds(384 * pair, 384)
+        copies.append(
+            pltpu.make_async_copy(rows.at[:, columns], out_ref.at[:, columns], sems.at[pair])
+        )
+        copies[-1].start()
+    for copy in copies:
+        copy.wait()
 
 
 def columns_of(row):
@@ -172,7 +181,7 @@
     )
 
 
-def spread_tokens(got_ref, slot_ref, out_ref):
+def spread_tokens(got_ref, slot_ref, out_ref, ready, sems):
     blocks = slot_ref.shape[0]
     owners = got_ref.shape[0]
     slots = owners * CAP
@@ -181,6 +190,7 @@
     tail = got_ref[:, 32:48, :].reshape(slots, 128)[:, 0:64]
     rows = jnp.concatenate([main, tail], axis=1)
     slot_f = slot_ref[...].astype(F32)
+    copies = []
     for u in range(blocks):
         mine = columns_of(slot_f[u : u + 1, :])
         pick = jnp.concatenate(
@@ -192,10 +202,14 @@
         )
         tokens = (jnp.dot(pick, rows, preferred_element_type=F32) * normalizer).astype(BF16)
         place = ROWS_ORDER.index(u)
-        out_ref[place, 0:128, :] = tokens[:, 0:128]
-        out_ref[place, 128:192, :] = jnp.concatenate(
+        ready[place, 0:128, :] = tokens[:, 0:128]
+        ready[place, 128:192, :] = jnp.concatenate(
             [tokens[0:64, 128:192], tokens[64:128, 128:192]], axis=1
         )
+        copies.append(pltpu.make_async_copy(ready.at[place], out_ref.at[place], sems.at[u]))
+        copies[-1].start()
+    for copy in copies:
+        copy.wait()
 
 
 def update_rows(me_ref, want_ref, got_ref, table_ref, moment_ref, new_table_ref, new_moment_ref):
@@ -283,7 +297,13 @@
         payload, "dp", split_axis=0, concat_axis=0, tiled=True, axis_index_groups=flipped
     )
     tokens = call(
-        spread_tokens, S((seq_count, 192, 128), BF16), 2, flops=2 * slots * blocks * 128 * 192, nbytes=1400000
+        spread_tokens,
+        S((seq_count, 192, 128), BF16),
+        2,
+        scratch=[pltpu.VMEM((seq_count, 192, 128), BF16), pltpu.SemaphoreType.DMA((blocks,))],
+        out_space=pl.ANY,
+        flops=2 * slots * blocks * 128 * 192,
+        nbytes=1400000,
     )(got, slot)
     arrived = lax.all_to_all(
         tokens, "seq", split_axis=0, concat_axis=0, tiled=True, axis_index_groups=[ROWS_ORDER]
@@ -296,7 +316,17 @@
         flops=2 * slots * owned * 192,
         nbytes=4000000,
     )(me, want, got, table, moment)
-    embedded = call(unpack_tokens, S((128, seq_count * 192), BF16), 1, nbytes=1200000)(arrived)
+    embedded = call(
+        unpack_tokens,
+        S((128, seq_count * 192), BF16),
+        1,
+        scratch=[
+            pltpu.VMEM((128, seq_count * 192), BF16),
+            pltpu.SemaphoreType.DMA((seq_count // 2,)),
+        ],
+        out_space=pl.ANY,
+        nbytes=1200000,
+    )(arrived)
     return embedded, new_table.T, new_moment.T
 
 

time: 121 us -> 121 us (level)
  no operation moved by 1% of the time
where the time goes in v3:
time: 121 us; the launch traced here: 120 us
  starting transfers between devices  48.9 us (40%)
  blocking collectives  32 us (26%)
  waiting for transfers between devices  22.2 us (18%)
  Pallas kernels  14.1 us (12%)
  local copies, waits for them, and re-layouts  1.76 us (1%)
    all_to_all x1, blocking collectives, local(): lax.all_to_all(payload, 'dp', split_axis=0, concat_axis=0, tiled=True, ax...  32 us
    ppermute x4, starting transfers between devices, exchange_requests(): got = lax.ppermute(want, 'dp', [(g, g ^ bit) for g in range(dp_count)])  19.1 us
    all_to_all x1, starting transfers between devices, local(): lax.all_to_all(packed, 'seq', split_axis=0, concat_axis=0, tiled=True, ax...  15.9 us
    all_to_all x1, waiting for transfers between devices, local(): lax.all_to_all(tokens, 'seq', split_axis=0, concat_axis=0, tiled=True, ax...  15.3 us
    all_to_all x1, starting transfers between devices, local(): lax.all_to_all(tokens, 'seq', split_axis=0, concat_axis=0, tiled=True, ax...  9.06 us
    all_to_all x1, starting transfers between devices, exchange_requests(): lax.all_to_all(want, 'dp', split_axis=0, concat_axis=0, tiled=True, axis_...  4.84 us
    ppermute x4, waiting for transfers between devices, exchange_requests(): got = lax.ppermute(want, 'dp', [(g, g ^ bit) for g in range(dp_count)])  4.82 us
    pallas_call x1, Pallas kernels, local(): call(update_rows, (S((192, owned), BF16), S((192, owned), BF16)), 5, smem...  4.41 us
  transfers between devices with their start and end apart: 7, of which 6 were waited for; matrix products, arithmetic and copies ran while one was open for 0% of the time, Pallas kernels for 6%

profile of v3, /device:TPU:1, one launch (start us, length us, event | category | flops | bytes accessed | tf_op | source)
XLA Modules:
  0.0 120.0 jit_solution(1633770831082702050)
XLA Ops:
  0.6 0.0 copy-start.1
  0.6 0.7 copy-done.1
  1.3 2.9 %shard_map.68 = (s32[12,128]{1,0:T(8,128)S(1)}, s32[4,2,128]{2,1,0:T(2,128)}) custom-call(s32[1]{0:T(128)} %bitcast.me_ref, s32[12,128]{1,0:T(8,128)S(1)} %bitcast.6), custom_call_target="tpu_custom_call" | custom-call | flops 1000000 | bytes 1000000 | tf_op jit(solution)/shard_map/pallas_call | solution.py:270
  4.3 4.8 %all-to-all-start.1 = ((s32[4,2,128]{2,1,0:T(2,128)}), s32[4,2,128]{2,1,0:T(2,128)S(1)}, u32[]{:S(2)}, u32[]{:S(2)}) async-start(s32[4,2,128]{2,1,0:T(2,128)} %get-tuple-element.8), calls=%async_computation.1 | async-start | bytes 8192 | tf_op jit(solution)/shard_map/all_to_all | solution.py:244
  9.1 0.0 copy-start
  9.1 1.1 copy-done
  10.2 1.0 shard_map.67
  11.2 0.0 copy-start.2
  11.2 2.0 %all-to-all-done.1 = s32[4,2,128]{2,1,0:T(2,128)S(1)} async-done(((s32[4,2,128]{2,1,0:T(2,128)}), s32[4,2,128]{2,1,0:T(2,128)S(1)}, u32[]{:S(2)}, u32[]{:S(2)}) %all-to-all-start.1) | async-done | bytes 4128 | tf_op jit(solution)/shard_map/all_to_all | solution.py:244
  13.3 15.9 %all-to-all-start = ((bf16[12,192,128]{2,1,0:T(8,128)(2,1)}), bf16[12,192,128]{2,1,0:T(8,128)(2,1)S(1)}, u32[]{:S(2)}, u32[]{:S(2)}) async-start(bf16[12,192,128]{2,1,0:T(8,128)(2,1)} %shard_map.67), calls=%async_computation | async-start | bytes 1179648 | tf_op jit(solution)/shard_map/all_to_all | solution.py:267
  29.1 4.3 %collective-permute-start = (s32[4,2,128]{2,1,0:T(2,128)S(1)}, s32[4,2,128]{2,1,0:T(2,128)S(1)}, u32[]{:S(2)}, u32[]{:S(2)}) collective-permute-start(s32[4,2,128]{2,1,0:T(2,128)S(1)} %all-to-all-done.1), channel_id=1, source_target_pairs={{0,12},{12,0},{24,36},{36,24},{48,60},{60,48},{72,84},{84,72},{96,... | collective-permute-start | bytes 12296 | tf_op jit(solution)/shard_map/ppermute | solution.py:249
  33.5 0.8 collective-permute-done
  34.2 0.1 compare_select_fusion
  34.3 3.2 %collective-permute-start.1 = (s32[4,2,128]{2,1,0:T(2,128)S(1)}, s32[4,2,128]{2,1,0:T(2,128)S(1)}, u32[]{:S(2)}, u32[]{:S(2)}) collective-permute-start(s32[4,2,128]{2,1,0:T(2,128)S(1)} %compare_select_fusion), channel_id=1, source_target_pairs={{0,24},{12,36},{24,0},{36,12},{48,72},{60,84},{72,48},{84,60},{96,... | collective-permute-start | bytes 12296 | tf_op jit(solution)/shard_map/ppermute | solution.py:249
  37.5 1.4 %collective-permute-done.1 = s32[4,2,128]{2,1,0:T(2,128)S(1)} collective-permute-done((s32[4,2,128]{2,1,0:T(2,128)S(1)}, s32[4,2,128]{2,1,0:T(2,128)S(1)}, u32[]{:S(2)}, u32[]{:S(2)}) %collective-permute-start.1) | collective-permute-done | bytes 4128 | tf_op jit(solution)/shard_map/ppermute | solution.py:249
  38.9 0.1 compare_select_fusion.1
  39.0 4.2 %collective-permute-start.2 = (s32[4,2,128]{2,1,0:T(2,128)S(1)}, s32[4,2,128]{2,1,0:T(2,128)S(1)}, u32[]{:S(2)}, u32[]{:S(2)}) collective-permute-start(s32[4,2,128]{2,1,0:T(2,128)S(1)} %compare_select_fusion.1), channel_id=1, source_target_pairs={{0,48},{12,60},{24,72},{36,84},{48,0},{60,12},{72,24},{84,36},{96,... | collective-permute-start | bytes 12296 | tf_op jit(solution)/shard_map/ppermute | solution.py:249
  43.2 1.3 %collective-permute-done.2 = s32[4,2,128]{2,1,0:T(2,128)S(1)} collective-permute-done((s32[4,2,128]{2,1,0:T(2,128)S(1)}, s32[4,2,128]{2,1,0:T(2,128)S(1)}, u32[]{:S(2)}, u32[]{:S(2)}) %collective-permute-start.2) | collective-permute-done | bytes 4128 | tf_op jit(solution)/shard_map/ppermute | solution.py:249
  44.6 0.1 compare_select_fusion.2
  44.6 7.4 %collective-permute-start.3 = (s32[4,2,128]{2,1,0:T(2,128)S(1)}, s32[4,2,128]{2,1,0:T(2,128)S(1)}, u32[]{:S(2)}, u32[]{:S(2)}) collective-permute-start(s32[4,2,128]{2,1,0:T(2,128)S(1)} %compare_select_fusion.2), channel_id=1, source_target_pairs={{0,96},{12,108},{24,120},{36,132},{48,144},{60,156},{72,168},{84,1... | collective-permute-start | bytes 12296 | tf_op jit(solution)/shard_map/ppermute | solution.py:249
  52.1 1.3 %collective-permute-done.3 = s32[4,2,128]{2,1,0:T(2,128)S(1)} collective-permute-done((s32[4,2,128]{2,1,0:T(2,128)S(1)}, s32[4,2,128]{2,1,0:T(2,128)S(1)}, u32[]{:S(2)}, u32[]{:S(2)}) %collective-permute-start.3) | collective-permute-done | bytes 4128 | tf_op jit(solution)/shard_map/ppermute | solution.py:249
  53.4 0.1 compare_select_fusion.3.want_ref
  53.4 0.0 copy-done.2
  53.4 1.5 %shard_map.69.rows_ref = bf16[1024,192]{1,0:T(8,128)(2,1)S(1)} custom-call(s32[1]{0:T(128)} %bitcast.me_ref, s32[4,2,128]{2,1,0:T(2,128)S(1)} %compare_select_fusion.3.want_ref, bf16[192,2000]{1,0:T(8,128)(2,1)S(1)} %bitcast.7), custom_call_target="tpu_custom_call" | custom-call | flops 786432000 | bytes 1200000 | tf_op jit(solution)/shard_map/pallas_call | solution.py:284
  55.0 0.0 all-to-all-done.cols_ref
  55.0 1.2 shard_map.70
  56.1 32.0 %all_to_all.20.got_ref = bf16[64,48,128]{2,1,0:T(8,128)(2,1)S(1)} all-to-all(bf16[64,48,128]{2,1,0:T(8,128)(2,1)S(1)} %shard_map.70), channel_id=1, replica_groups={{96,108,120,132,144,156,168,180,0,12,24,36,48,60,72,84,288,300,312,324,..., dimensions={0} | all-to-all | bytes 1572864 | tf_op jit(solution)/shard_map/all_to_all | solution.py:296
  88.1 1.8 %shard_map.71 = bf16[12,192,128]{2,1,0:T(8,128)(2,1)} custom-call(bf16[64,48,128]{2,1,0:T(8,128)(2,1)S(1)} %all_to_all.20.got_ref, s32[12,128]{1,0:T(8,128)S(1)} %get-tuple-element.7.slot_ref), custom_call_target="tpu_custom_call" | custom-call | flops 603979776 | bytes 1400000 | tf_op jit(solution)/shard_map/pallas_call | solution.py:299
  89.9 0.0 copy-start.3
  90.0 9.1 %all-to-all-start.3 = ((bf16[12,192,128]{2,1,0:T(8,128)(2,1)}), bf16[12,192,128]{2,1,0:T(8,128)(2,1)S(1)}, u32[]{:S(2)}, u32[]{:S(2)}) async-start(bf16[12,192,128]{2,1,0:T(8,128)(2,1)} %shard_map.71), calls=%async_computation.3 | async-start | bytes 1179648 | tf_op jit(solution)/shard_map/all_to_all | solution.py:308
  99.0 0.0 copy-done.3
  99.0 4.4 %shard_map.73 = (bf16[192,2000]{1,0:T(8,128)(2,1)}, bf16[192,2000]{1,0:T(8,128)(2,1)}) custom-call(s32[1]{0:T(128)} %bitcast.me_ref, s32[4,2,128]{2,1,0:T(2,128)S(1)} %compare_select_fusion.3.want_ref, bf16[64,48,128]{2,1,0:T(8,128)(2,1)S(1)} %all_to_all.20.got_ref, bf16[192,2000]{1,0:T(8,128)(2,1)S(1)} %bitcast.8, bf16[192,2000]{1,0:T(8,128)(2,1)S(1)} %bitcast.9), custom_call_target="tpu_custom_call" | custom-call | flops 786432000 | bytes 4000000 | tf_op jit(solution)/shard_map/pallas_call | solution.py:311
  103.4 15.3 %all-to-all-done.3.in_ref = bf16[12,192,128]{2,1,0:T(8,128)(2,1)S(1)} async-done(((bf16[12,192,128]{2,1,0:T(8,128)(2,1)}), bf16[12,192,128]{2,1,0:T(8,128)(2,1)S(1)}, u32[]{:S(2)}, u32[]{:S(2)}) %all-to-all-start.3) | async-done | bytes 589856 | tf_op jit(solution)/shard_map/all_to_all | solution.py:308
  118.8 1.2 %shard_map.72 = bf16[128,2304]{1,0:T(8,128)(2,1)} custom-call(bf16[12,192,128]{2,1,0:T(8,128)(2,1)S(1)} %all-to-all-done.3.in_ref), custom_call_target="tpu_custom_call" | custom-call | bytes 1200000 | tf_op jit(solution)/shard_map/pallas_call | solution.py:319
  (4 shorter events, 0.0 us)
Async XLA Ops:
  0.6 0.7 copy-start.1
  4.3 9.0 %all-to-all-start.1 = ((s32[4,2,128]{2,1,0:T(2,128)}), s32[4,2,128]{2,1,0:T(2,128)S(1)}, u32[]{:S(2)}, u32[]{:S(2)}) async-start(s32[4,2,128]{2,1,0:T(2,128)} %get-tuple-element.8), calls=%async_computation.1 | async-start | bytes 8192 | tf_op jit(solution)/shard_map/all_to_all | solution.py:244
  9.1 1.1 copy-start
  11.2 42.2 %copy-start.2 = (bf16[2000,192]{0,1:T(8,128)(2,1)S(1)}, bf16[2000,192]{0,1:T(8,128)(2,1)}, u32[]{:S(2)}) copy-start(bf16[2000,192]{0,1:T(8,128)(2,1)} %param.5) | copy-start | bytes 2304004
  13.3 41.7 %all-to-all-start = ((bf16[12,192,128]{2,1,0:T(8,128)(2,1)}), bf16[12,192,128]{2,1,0:T(8,128)(2,1)S(1)}, u32[]{:S(2)}, u32[]{:S(2)}) async-start(bf16[12,192,128]{2,1,0:T(8,128)(2,1)} %shard_map.67), calls=%async_computation | async-start | bytes 1179648 | tf_op jit(solution)/shard_map/all_to_all | solution.py:267
  29.1 5.1 %collective-permute-start = (s32[4,2,128]{2,1,0:T(2,128)S(1)}, s32[4,2,128]{2,1,0:T(2,128)S(1)}, u32[]{:S(2)}, u32[]{:S(2)}) collective-permute-start(s32[4,2,128]{2,1,0:T(2,128)S(1)} %all-to-all-done.1), channel_id=1, source_target_pairs={{0,12},{12,0},{24,36},{36,24},{48,60},{60,48},{72,84},{84,72},{96,... | collective-permute-start | bytes 12296 | tf_op jit(solution)/shard_map/ppermute | solution.py:249
  34.3 4.6 %collective-permute-start.1 = (s32[4,2,128]{2,1,0:T(2,128)S(1)}, s32[4,2,128]{2,1,0:T(2,128)S(1)}, u32[]{:S(2)}, u32[]{:S(2)}) collective-permute-start(s32[4,2,128]{2,1,0:T(2,128)S(1)} %compare_select_fusion), channel_id=1, source_target_pairs={{0,24},{12,36},{24,0},{36,12},{48,72},{60,84},{72,48},{84,60},{96,... | collective-permute-start | bytes 12296 | tf_op jit(solution)/shard_map/ppermute | solution.py:249
  39.0 5.5 %collective-permute-start.2 = (s32[4,2,128]{2,1,0:T(2,128)S(1)}, s32[4,2,128]{2,1,0:T(2,128)S(1)}, u32[]{:S(2)}, u32[]{:S(2)}) collective-permute-start(s32[4,2,128]{2,1,0:T(2,128)S(1)} %compare_select_fusion.1), channel_id=1, source_target_pairs={{0,48},{12,60},{24,72},{36,84},{48,0},{60,12},{72,24},{84,36},{96,... | collective-permute-start | bytes 12296 | tf_op jit(solution)/shard_map/ppermute | solution.py:249
  44.6 8.7 %collective-permute-start.3 = (s32[4,2,128]{2,1,0:T(2,128)S(1)}, s32[4,2,128]{2,1,0:T(2,128)S(1)}, u32[]{:S(2)}, u32[]{:S(2)}) collective-permute-start(s32[4,2,128]{2,1,0:T(2,128)S(1)} %compare_select_fusion.2), channel_id=1, source_target_pairs={{0,96},{12,108},{24,120},{36,132},{48,144},{60,156},{72,168},{84,1... | collective-permute-start | bytes 12296 | tf_op jit(solution)/shard_map/ppermute | solution.py:249
  89.9 9.1 %copy-start.3 = (bf16[2000,192]{0,1:T(8,128)(2,1)S(1)}, bf16[2000,192]{0,1:T(8,128)(2,1)}, u32[]{:S(2)}) copy-start(bf16[2000,192]{0,1:T(8,128)(2,1)} %param.6) | copy-start | bytes 2304004
  90.0 28.8 %all-to-all-start.3 = ((bf16[12,192,128]{2,1,0:T(8,128)(2,1)}), bf16[12,192,128]{2,1,0:T(8,128)(2,1)S(1)}, u32[]{:S(2)}, u32[]{:S(2)}) async-start(bf16[12,192,128]{2,1,0:T(8,128)(2,1)} %shard_map.71), calls=%async_computation.3 | async-start | bytes 1179648 | tf_op jit(solution)/shard_map/all_to_all | solution.py:308
